TPU v7x, 32 devices: a whole 2x2x4 slice. The times are simulated.
32 devices in a mesh: ifg: 16 (over z, y, x), tile: 2 (over core).
Axes of the slice: x: 2, y: 2, z: 4, core: 2. Of those that a mesh axis runs over, the one named last changes fastest.
Arguments:
- phases: float32 [1024, 128, 64], P('ifg', 'tile'), may hold values from -6 to 6
- pairs: int32 [1024, 2], replicated, may hold values from 0 to 299, as said below
- class_weights: float32 [8, 1024], replicated, may hold values from 0.05 to 1
- classes: int32 [128, 64], P('tile', 'ifg'), may hold values from 0 to 7
Outputs:
- corrected: float32 [128, 64, 300], P('tile', 'ifg')
Inputs may be any that keep to these rules, and one draw needn't show every extreme that they name: pairs[i,0] < pairs[i,1] <= pairs[i,0] + 8; some interferogram starts at date 0 and some ends at date 300 - 1.
All inputs are finite; a program needn't handle non-finite values.
Results may differ from a plain program's by a relative error of at most 0.0003.
Values sent between devices are 32-bit elements; how exact they have to be, the bound alone decides.
A program may use at most 128 MiB of HBM per device.

v0:
```python
import jax
import jax.numpy as jnp
from jax import lax
from jax.sharding import PartitionSpec as P

DATES = 300
CLASSES = 8
MAXGAP = 8
R = 3
smooth_weight = 1.0
anchor_weight = 0.1


def with_halo(cells, sides, width):
    for axis, dim in sides:
        count = lax.axis_size(axis)
        ends = count - 1
        head = lax.slice_in_dim(cells, 0, width, axis=dim)
        tail = lax.slice_in_dim(cells, cells.shape[dim] - width, cells.shape[dim], axis=dim)
        cells = jnp.concatenate(
            [
                lax.ppermute(tail, axis, [(i, (i + 1) % count) for i in range(ends)]),
                cells,
                lax.ppermute(head, axis, [((i + 1) % count, i) for i in range(ends)]),
            ],
            axis=dim,
        )
    return cells


def incidence_matrix(pairs):
    dates = jnp.arange(DATES, dtype=jnp.int32)[:, None]
    plus = (dates == pairs[:, 1][None, :]).astype(jnp.float32)
    minus = (dates == pairs[:, 0][None, :]).astype(jnp.float32)
    return (plus, minus)


def prior_matrix():
    second = jnp.arange(DATES - 2, dtype=jnp.int32)[:, None]
    columns = jnp.arange(DATES, dtype=jnp.int32)[None, :]
    diffs = (
        (columns == second).astype(jnp.float32)
        - 2.0 * (columns == second + 1).astype(jnp.float32)
        + (columns == second + 2).astype(jnp.float32)
    )
    curvature = jnp.dot(
        diffs.T, diffs, precision=lax.Precision.HIGHEST, preferred_element_type=jnp.float32
    )
    return smooth_weight * curvature + anchor_weight * jnp.eye(DATES, dtype=jnp.float32)


def class_systems(pairs, plus, minus, weights):
    diagonal = jnp.dot(
        weights,
        (plus + minus).T,
        precision=lax.Precision.HIGHEST,
        preferred_element_type=jnp.float32,
    )
    spacing = pairs[:, 1] - pairs[:, 0]
    offsets = jnp.arange(1, MAXGAP + 1, dtype=jnp.int32)[:, None]
    gap_onehot = (spacing[None, :] == offsets).astype(jnp.float32)
    spread = weights[:, None, :] * gap_onehot[None, :, :]
    band = jnp.einsum("kgi,ai->kga", spread, minus, precision=lax.Precision.HIGHEST)
    row_ids = jnp.arange(DATES, dtype=jnp.int32)[:, None]
    col_ids = jnp.arange(DATES, dtype=jnp.int32)[None, :]
    normal = diagonal[:, :, None] * (row_ids == col_ids).astype(jnp.float32)[None]
    for offset in range(MAXGAP):
        select = (col_ids == row_ids + offset + 1).astype(jnp.float32)
        normal = (
            normal
            - band[:, offset, :, None] * select[None]
            - band[:, offset, None, :] * select.T[None]
        )
    return normal


def invert(matrix):
    factor = jnp.linalg.cholesky(matrix)
    return jax.scipy.linalg.cho_solve((factor, True), jnp.eye(DATES, dtype=jnp.float32))


def filter_taps():
    offsets = jnp.arange(-R, R + 1).astype(jnp.float32)
    values = jnp.exp(-offsets * offsets / 4.5)
    return values / jnp.sum(values)


def pass_columns(padded, filter_weights, width):
    result = filter_weights[0] * padded[:, 0:width]
    for offset in range(1, 2 * R + 1):
        result = result + filter_weights[offset] * padded[:, offset : offset + width]
    return result


def pass_rows(padded, filter_weights, height):
    result = filter_weights[0] * padded[0:height]
    for offset in range(1, 2 * R + 1):
        result = result + filter_weights[offset] * padded[offset : offset + height]
    return result


def date_terms(received, incidence, weight_rows, onehot):
    flat = received.reshape(received.shape[0], -1)
    pixel_weights = jnp.dot(
        weight_rows, onehot, precision=lax.Precision.HIGHEST, preferred_element_type=jnp.float32
    )
    return jnp.einsum("ip,di->pd", pixel_weights * flat, incidence, precision=lax.Precision.HIGHEST)


def on_device(phases, pairs, class_weights, classes):
    plus, minus = incidence_matrix(pairs)
    incidence = plus - minus
    class_share = CLASSES // lax.axis_size("tile")
    first_class = lax.axis_index("tile") * class_share
    own_weights = lax.dynamic_slice_in_dim(class_weights, first_class, class_share, 0)
    own_normal = class_systems(pairs, plus, minus, own_weights)
    own_inverse = jax.vmap(invert)(own_normal + prior_matrix()[None])
    inverse = lax.all_gather(own_inverse, "tile", axis=0, tiled=True)
    tile_rows = phases.shape[1]
    tile_cols = classes.shape[1]
    class_flat = classes.reshape(-1)
    onehot = (class_flat[None, :] == jnp.arange(CLASSES, dtype=jnp.int32)[:, None]).astype(
        jnp.float32
    )
    weight_rows = class_weights.T
    regrouped = lax.all_to_all(phases, "ifg", split_axis=2, concat_axis=0, tiled=True)
    right_terms = date_terms(regrouped, incidence, weight_rows, onehot)
    solution = jnp.zeros((tile_rows * tile_cols, DATES), jnp.float32)
    for member in range(CLASSES):
        solved = jnp.einsum(
            "pd,ed->pe", right_terms, inverse[member], precision=lax.Precision.HIGHEST
        )
        solution = solution + onehot[member][:, None] * solved
    displacement = solution.reshape(tile_rows, tile_cols, DATES)
    filter_weights = filter_taps()
    padded = with_halo(displacement, (("ifg", 1), ("tile", 0)), R)
    across = pass_columns(padded, filter_weights, tile_cols)
    atmosphere = pass_rows(across, filter_weights, tile_rows)
    return displacement - atmosphere


def solution(mesh):
    return jax.shard_map(
        on_device,
        mesh=mesh,
        in_specs=(P("ifg", "tile", None), P(), P(), P("tile", "ifg")),
        out_specs=P("tile", "ifg", None),
        check_vma=False,
    )
```

profile of v0, /device:TPU:13, one launch (start us, length us, event | category | flops | bytes accessed | tf_op | source)
XLA Modules:
  0.0 464.6 jit_solution(6404731645494615155)
XLA Ops:
  12.6 4.8 %fusion.2 = f32[4,300,300]{2,1,0:T(8,128)S(1)} fusion(f32[300,300]{1,0:T(8,128)S(1)} %copy.75, f32[300,300]{1,0:T(8,128)S(1)} %copy.74, f32[4,300]{1,0:T(4,128)S(1)} %fusion.6, f32[300,300]{1,0:T(8,128)S(1)} %copy.73, f32[300,300]{1,0:T(8,128)S(1)} %get-tuple-element.96, f32[4,300]{1,0:T(4,128)S(1)} %get-tuple-element.82, ...), kind=kLoop, calls=%fused_computation.36 | loop fusion | flops 19440000 | bytes 8683200 | tf_op jit(solution)/shard_map/vmap(jit(cholesky))/div | solution.py:78
  18.7 46.9 %custom-call.29 = f32[4,128,128]{2,1,0:T(8,128)S(1)} custom-call(f32[4,128,128]{2,1,0:T(8,128)S(1)} %cholesky.205), custom_call_target="Cholesky" | custom-call | tf_op jit(solution)/shard_map/vmap(jit(cholesky))/cholesky | solution.py:78
  65.8 39.9 %custom-call.30 = f32[4,1,128,128]{2,3,1,0:T(8,128)} custom-call(f32[4,1,128,128]{3,2,1,0:T(8,128)S(1)} %select_bitcast_fusion.1), custom_call_target="InvertDiagBlocksLowerTriangular" | custom-call | tf_op jit(solution)/shard_map/vmap(jit(cholesky))/cholesky | solution.py:78
  109.6 48.5 %custom-call.31 = f32[4,128,128]{2,1,0:T(8,128)} custom-call(f32[4,128,128]{2,1,0:T(8,128)} %cholesky.209), custom_call_target="Cholesky" | custom-call | tf_op jit(solution)/shard_map/vmap(jit(cholesky))/cholesky | solution.py:78
  159.8 40.1 %custom-call.32 = f32[4,1,128,128]{2,3,1,0:T(8,128)S(1)} custom-call(f32[4,1,128,128]{3,2,1,0:T(8,128)} %get-tuple-element.31), custom_call_target="InvertDiagBlocksLowerTriangular" | custom-call | tf_op jit(solution)/shard_map/vmap(jit(cholesky))/cholesky | solution.py:78
  201.5 16.1 %custom-call.33 = f32[4,44,44]{2,1,0:T(8,128)S(1)} custom-call(f32[4,44,44]{2,1,0:T(8,128)S(1)} %convolution_subtract_fusion.4), custom_call_target="Cholesky" | custom-call | tf_op jit(solution)/shard_map/vmap(jit(cholesky))/cholesky | solution.py:78
  220.8 4.1 while.1
  225.1 118.7 %custom-call.34 = f32[4,3,128,128]{2,3,1,0:T(8,128)} custom-call(f32[4,3,128,128]{3,2,1,0:T(8,128)S(1)} %pad_maximum_fusion.2), custom_call_target="InvertDiagBlocksLowerTriangular" | custom-call | tf_op jit(solution)/shard_map/vmap(jit(_cho_solve))/triangular_solve | solution.py:79
  351.9 2.0 convolution_subtract_fusion.1
  360.8 3.1 copy.69
  363.9 2.3 reshape.539
  366.2 6.9 %all-to-all-start = ((f32[16,1,16384]{2,1,0:T(1,128)}), f32[16,1,16384]{2,1,0:T(1,128)S(1)}, u32[]{:S(2)}, u32[]{:S(2)}) async-start(f32[16,1,16384]{2,1,0:T(1,128)} %reshape.539), calls=%async_computation | async-start | bytes 2097152 | tf_op jit(solution)/shard_map/all_to_all | solution.py:126
  373.4 24.5 %all-to-all-done = f32[16,1,16384]{2,1,0:T(1,128)S(1)} async-done(((f32[16,1,16384]{2,1,0:T(1,128)}), f32[16,1,16384]{2,1,0:T(1,128)S(1)}, u32[]{:S(2)}, u32[]{:S(2)}) %all-to-all-start) | async-done | bytes 1048608 | tf_op jit(solution)/shard_map/all_to_all | solution.py:126
  398.4 3.1 reduce.18
  402.4 2.7 copy.70
  405.1 2.0 reshape.515
  409.2 1.8 convolution_multiply_fusion.6
  419.3 2.1 collective-permute-start
  421.5 4.1 collective-permute-start.1
  426.8 4.2 collective-permute-done
  431.0 10.1 %collective-permute-done.1 = f32[64,3,300]{2,1,0:T(4,128)S(1)} collective-permute-done((f32[64,3,300]{2,1,0:T(4,128)S(1)}, f32[64,3,300]{2,1,0:T(4,128)S(1)}, u32[]{:S(2)}, u32[]{:S(2)}) %collective-permute-start.1) | collective-permute-done | bytes 230432 | tf_op jit(solution)/shard_map/ppermute | solution.py:24
  442.4 3.0 collective-permute-start.3
  446.8 5.0 %fusion.56 = f32[70,4,300]{2,1,0:T(4,128)S(1)} fusion(f32[70,10,300]{2,1,0:T(8,128)S(1)} %pad_maximum_fusion.1, f32[]{:T(128)} %bitcast.39, f32[]{:T(128)} %bitcast.38, f32[]{:T(128)} %bitcast.37, f32[]{:T(128)} %bitcast.36, f32[]{:T(128)} %bitcast.35, f32[]{:T(128)} %bitcast.34, f32[]{:T(128)} %bitcast.33), kind=kLoop, calls=%fused_computation.143 | loop fusion | flops 1092000 | bytes 2688028 | tf_op jit(solution)/shard_map/add | solution.py:91
  451.8 5.5 %fusion.63 = f32[64,4,300]{2,1,0:T(4,128)} fusion(f32[64,4,300]{2,1,0:T(4,128)S(1)} %reshape.516, f32[70,4,300]{2,1,0:T(4,128)S(1)} %fusion.56, f32[]{:T(128)} %bitcast.39, f32[]{:T(128)} %bitcast.38, f32[]{:T(128)} %bitcast.37, f32[]{:T(128)} %bitcast.36, f32[]{:T(128)} %bitcast.35, f32[]{:T(128)} %bitcast.34, f32[]{:T(128)} %bitcast.33), kind=kLoop, calls=%fused_computation.157 | loop fusion | flops 1075200 | bytes 2764828 | tf_op jit(solution)/shard_map/sub | solution.py:139
  (126 shorter events, 52.3 us)
Async XLA Ops:
  6.5 0.8 copy-start
  6.5 0.7 copy-start.5
  6.5 402.6 %all-gather.2.cloned.1.call-start = ((), (), s32[]{:S(2)}) async-start(), calls=%async_computation.1 | async-start | bytes 5603328 | tf_op jit(solution)/shard_map/all_gather | solution.py:118
  6.7 2.7 copy-start.3
  17.4 1.3 copy-start.2
  217.7 1.3 copy-start.1
  343.9 4.0 slice-start
  363.9 9.3 %copy-start.6 = (s32[64,4]{0,1:T(4,128)S(1)}, s32[64,4]{0,1:T(4,128)}, u32[]{:S(2)}) copy-start(s32[64,4]{0,1:T(4,128)} %param.7) | copy-start | bytes 3076
  366.2 31.7 %all-to-all-start = ((f32[16,1,16384]{2,1,0:T(1,128)}), f32[16,1,16384]{2,1,0:T(1,128)S(1)}, u32[]{:S(2)}, u32[]{:S(2)}) async-start(f32[16,1,16384]{2,1,0:T(1,128)} %reshape.539), calls=%async_computation | async-start | bytes 2097152 | tf_op jit(solution)/shard_map/all_to_all | solution.py:126
  409.2 6.9 %copy-start.4 = (f32[8,300,300]{2,1,0:T(8,128)S(1)}, f32[8,300,300]{2,1,0:T(8,128)}, u32[]{:S(2)}) copy-start(f32[8,300,300]{2,1,0:T(8,128)} %all-gather.2.cloned.1.call-done) | copy-start | bytes 8640004
  419.3 11.7 %collective-permute-start = (f32[64,3,300]{2,1,0:T(4,128)S(1)}, f32[64,3,300]{2,1,0:T(4,128)S(1)}, u32[]{:S(2)}, u32[]{:S(2)}) collective-permute-start(f32[64,3,300]{2,1,0:T(4,128)S(1)} %get-tuple-element.29), channel_id=1, source_target_pairs={{0,2},{2,4},{4,6},{6,8},{8,10},{10,12},{12,14},{14,16},{16,18},{18... | collective-permute-start | bytes 691208 | tf_op jit(solution)/shard_map/ppermute | solution.py:22
  421.5 19.6 %collective-permute-start.1 = (f32[64,3,300]{2,1,0:T(4,128)S(1)}, f32[64,3,300]{2,1,0:T(4,128)S(1)}, u32[]{:S(2)}, u32[]{:S(2)}) collective-permute-start(f32[64,3,300]{2,1,0:T(4,128)S(1)} %get-tuple-element.30), channel_id=1, source_target_pairs={{2,0},{4,2},{6,4},{8,6},{10,8},{12,10},{14,12},{16,14},{18,16},{20... | collective-permute-start | bytes 691208 | tf_op jit(solution)/shard_map/ppermute | solution.py:24
  441.1 5.0 %collective-permute-start.2 = (f32[3,10,300]{2,1,0:T(8,128)S(1)}, f32[3,10,300]{2,1,0:T(8,128)S(1)}, u32[]{:S(2)}, u32[]{:S(2)}) collective-permute-start(f32[3,10,300]{2,1,0:T(8,128)S(1)} %get-tuple-element.25), channel_id=1, source_target_pairs={{0,1},{2,3},{4,5},{6,7},{8,9},{10,11},{12,13},{14,15},{16,17},{18,... | collective-permute-start | bytes 108008 | tf_op jit(solution)/shard_map/ppermute | solution.py:22
  442.4 3.9 collective-permute-start.3
Sparse Core Ops, SparseCore 0:
  360.9 14.8 all-gather.1
where the time goes:
time: 470 us; the launch traced here: 465 us
  other arithmetic  336 us (71%)
  waiting for transfers between devices  39 us (8%)
  matrix products  34.2 us (7%)
  local copies, waits for them, and re-layouts  23.4 us (5%)
  starting transfers between devices  17.5 us (4%)
  between operations  14.6 us (3%)
    another operation x14, other arithmetic, invert(): factor = jnp.linalg.cholesky(matrix)  194 us
    another operation x9, other arithmetic, invert(): jax.scipy.linalg.cho_solve((factor, True), jnp.eye(DATES, dtype=jnp.float...  121 us
    all_to_all x1, waiting for transfers between devices, on_device(): lax.all_to_all(phases, 'ifg', split_axis=2, concat_axis=0, tiled=True)  24.5 us
    another operation x10, matrix products, invert(): jax.scipy.linalg.cho_solve((factor, True), jnp.eye(DATES, dtype=jnp.float...  14.5 us
    ppermute x2, waiting for transfers between devices, with_halo(): lax.ppermute(head, axis, [((i + 1) % count, i) for i in range(ends)])  10.3 us
    dot_general x8, matrix products, on_device(): jnp.einsum('pd,ed->pe', right_terms, inverse[member], precision=lax.Preci...  9.61 us
  transfers between devices with their start and end apart: 6, of which 4 were waited for; matrix products, arithmetic and copies ran while one was open for 4% of the time, Pallas kernels for 0%

commit v1 on v0

--- a/solution.py
+++ b/solution.py
@@ -123,7 +123,9 @@
         jnp.float32
     )
     weight_rows = class_weights.T
-    regrouped = lax.all_to_all(phases, "ifg", split_axis=2, concat_axis=0, tiled=True)
+    pieces = jnp.split(phases, lax.axis_size("ifg"), axis=2)
+    incoming = lax.all_to_all(jnp.stack(pieces), "ifg", 0, 0)
+    regrouped = jnp.concatenate(incoming, axis=0)
     right_terms = date_terms(regrouped, incidence, weight_rows, onehot)
     solution = jnp.zeros((tile_rows * tile_cols, DATES), jnp.float32)
     for member in range(CLASSES):

time: 470 us -> 536 us (1.14)
  local copies, waits for them, and re-layouts: 23.4 us -> 86.8 us
    unnamed x22 -> x66, local copies, waits for them, and re-layouts: 8.7 us -> 53.9 us
    split x0 -> x1, local copies, waits for them, and re-layouts: none -> 15.2 us  [on_device(): pieces = jnp.split(phases, lax.axis_size('ifg'), axis=2)]
  transfers between devices with their start and end apart: 6 -> 6, of which waited for: 4 -> 3; matrix products, arithmetic and copies ran while one was open for 4% -> 15% of each run, Pallas kernels for 0% -> 0%
where the time goes in v1:
time: 536 us; the launch traced here: 530 us
  other arithmetic  337 us (63%)
  local copies, waits for them, and re-layouts  86.8 us (16%)
  waiting for transfers between devices  38.4 us (7%)
  matrix products  35 us (7%)
  starting transfers between devices  17.8 us (3%)
  between operations  14.4 us (3%)
    another operation x14, other arithmetic, invert(): factor = jnp.linalg.cholesky(matrix)  194 us
    another operation x9, other arithmetic, invert(): jax.scipy.linalg.cho_solve((factor, True), jnp.eye(DATES, dtype=jnp.float...  122 us
    unnamed x66, local copies, waits for them, and re-layouts  53.9 us
    all_to_all x1, waiting for transfers between devices, on_device(): incoming = lax.all_to_all(jnp.stack(pieces), 'ifg', 0, 0)  24.6 us
    split x1, local copies, waits for them, and re-layouts, on_device(): pieces = jnp.split(phases, lax.axis_size('ifg'), axis=2)  15.2 us
    another operation x10, matrix products, invert(): jax.scipy.linalg.cho_solve((factor, True), jnp.eye(DATES, dtype=jnp.float...  14.5 us
    ppermute x2, waiting for transfers between devices, with_halo(): lax.ppermute(head, axis, [((i + 1) % count, i) for i in range(ends)])  12.6 us
  transfers between devices with their start and end apart: 6, of which 3 were waited for; matrix products, arithmetic and copies ran while one was open for 15% of the time, Pallas kernels for 0%

profile of v1, /device:TPU:13, one launch (start us, length us, event | category | flops | bytes accessed | tf_op | source)
XLA Modules:
  0.0 529.9 jit_solution(12543109315003079016)
XLA Ops:
  14.4 4.5 fusion.2
  20.2 46.9 %custom-call.29 = f32[4,128,128]{2,1,0:T(8,128)S(1)} custom-call(f32[4,128,128]{2,1,0:T(8,128)S(1)} %cholesky.205), custom_call_target="Cholesky" | custom-call | tf_op jit(solution)/shard_map/vmap(jit(cholesky))/cholesky | solution.py:78
  67.2 39.9 %custom-call.30 = f32[4,1,128,128]{2,3,1,0:T(8,128)} custom-call(f32[4,1,128,128]{3,2,1,0:T(8,128)S(1)} %select_bitcast_fusion.1), custom_call_target="InvertDiagBlocksLowerTriangular" | custom-call | tf_op jit(solution)/shard_map/vmap(jit(cholesky))/cholesky | solution.py:78
  111.1 48.5 %custom-call.31 = f32[4,128,128]{2,1,0:T(8,128)} custom-call(f32[4,128,128]{2,1,0:T(8,128)} %cholesky.209), custom_call_target="Cholesky" | custom-call | tf_op jit(solution)/shard_map/vmap(jit(cholesky))/cholesky | solution.py:78
  161.3 40.1 %custom-call.32 = f32[4,1,128,128]{2,3,1,0:T(8,128)S(1)} custom-call(f32[4,1,128,128]{3,2,1,0:T(8,128)} %get-tuple-element.47), custom_call_target="InvertDiagBlocksLowerTriangular" | custom-call | tf_op jit(solution)/shard_map/vmap(jit(cholesky))/cholesky | solution.py:78
  203.0 16.1 %custom-call.33 = f32[4,44,44]{2,1,0:T(8,128)S(1)} custom-call(f32[4,44,44]{2,1,0:T(8,128)S(1)} %convolution_subtract_fusion.4), custom_call_target="Cholesky" | custom-call | tf_op jit(solution)/shard_map/vmap(jit(cholesky))/cholesky | solution.py:78
  222.3 3.9 while.1
  226.5 118.9 %custom-call.34 = f32[4,3,128,128]{2,3,1,0:T(8,128)} custom-call(f32[4,3,128,128]{3,2,1,0:T(8,128)S(1)} %pad_maximum_fusion.2), custom_call_target="InvertDiagBlocksLowerTriangular" | custom-call | tf_op jit(solution)/shard_map/vmap(jit(_cho_solve))/triangular_solve | solution.py:79
  361.9 3.0 copy.118
  364.9 15.2 %fusion.105 = (f32[64,64,4]{2,1,0:T(8,128)}, f32[64,64,4]{2,1,0:T(8,128)}, f32[64,64,4]{2,1,0:T(8,128)}, f32[64,64,4]{2,1,0:T(8,128)}, f32[64,64,4]{2,1,0:T(8,12...) fusion(f32[64,64,64]{2,1,0:T(8,128)S(1)} %copy-done.1), kind=kLoop, calls=%fused_computation.271 | loop fusion | bytes 2097152 | tf_op jit(solution)/shard_map/split | solution.py:126
  383.1 3.1 copy.139
  386.2 2.9 copy.140
  390.4 3.1 copy.142
  393.5 2.9 copy.143
  428.0 3.5 reshape.534
  431.4 6.6 %all-to-all-start = ((f32[16,1,16384]{2,1,0:T(1,128)}), f32[16,1,16384]{2,1,0:T(1,128)S(1)}, u32[]{:S(2)}, u32[]{:S(2)}) async-start(f32[16,1,16384]{2,1,0:T(1,128)} %reshape.534), calls=%async_computation | async-start | bytes 2097152 | tf_op jit(solution)/shard_map/all_to_all | solution.py:127
  438.3 24.6 %all-to-all-done = f32[16,1,16384]{2,1,0:T(1,128)S(1)} async-done(((f32[16,1,16384]{2,1,0:T(1,128)}), f32[16,1,16384]{2,1,0:T(1,128)S(1)}, u32[]{:S(2)}, u32[]{:S(2)}) %all-to-all-start) | async-done | bytes 1048608 | tf_op jit(solution)/shard_map/all_to_all | solution.py:127
  463.4 3.1 reduce.18
  467.4 2.7 copy.99
  486.4 3.4 collective-permute-start
  491.1 12.6 %collective-permute-done.1 = f32[64,3,300]{2,1,0:T(4,128)S(1)} collective-permute-done((f32[64,3,300]{2,1,0:T(4,128)S(1)}, f32[64,3,300]{2,1,0:T(4,128)S(1)}, u32[]{:S(2)}, u32[]{:S(2)}) %collective-permute-start.1) | collective-permute-done | bytes 230432 | tf_op jit(solution)/shard_map/ppermute | solution.py:24
  503.7 4.6 collective-permute-start.3
  511.9 5.2 fusion.56
  517.2 5.7 %fusion.63 = f32[64,4,300]{2,1,0:T(4,128)} fusion(f32[64,4,300]{2,1,0:T(4,128)S(1)} %reshape.511, f32[70,4,300]{2,1,0:T(4,128)S(1)} %fusion.56, f32[]{:T(128)} %bitcast.53, f32[]{:T(128)} %bitcast.52, f32[]{:T(128)} %bitcast.51, f32[]{:T(128)} %bitcast.50, f32[]{:T(128)} %bitcast.49, f32[]{:T(128)} %bitcast.48, f32[]{:T(128)} %bitcast.47), kind=kLoop, calls=%fused_computation.157 | loop fusion | flops 1075200 | bytes 2764828 | tf_op jit(solution)/shard_map/sub | solution.py:141
  (172 shorter events, 98.3 us)
Async XLA Ops:
  6.5 3.4 copy-start
  6.5 0.7 copy-start.12
  6.5 467.8 %all-gather.2.cloned.1.call-start = ((), (), s32[]{:S(2)}) async-start(), calls=%async_computation.1 | async-start | bytes 5603328 | tf_op jit(solution)/shard_map/all_gather | solution.py:118
  6.6 2.9 copy-start.10
  18.9 1.3 copy-start.9
  219.2 1.3 copy-start.7
  345.5 4.0 slice-start
  349.5 2.7 copy-start.8
  361.9 3.0 copy-start.1
  383.1 6.0 %copy-start.6 = (f32[64,64,4]{2,1,0:T(8,128)S(1)}, f32[64,64,4]{2,1,0:T(8,128)}, u32[]{:S(2)}) copy-start(f32[64,64,4]{2,1,0:T(8,128)} %get-tuple-element.37) | copy-start | bytes 196612
  390.4 6.0 %copy-start.5 = (f32[64,64,4]{2,1,0:T(8,128)S(1)}, f32[64,64,4]{2,1,0:T(8,128)}, u32[]{:S(2)}) copy-start(f32[64,64,4]{2,1,0:T(8,128)} %get-tuple-element.34) | copy-start | bytes 196612
  397.1 4.8 copy-start.4
  402.6 4.8 copy-start.3
  408.1 4.8 copy-start.2
  428.0 10.1 %copy-start.13 = (s32[64,4]{0,1:T(4,128)S(1)}, s32[64,4]{0,1:T(4,128)}, u32[]{:S(2)}) copy-start(s32[64,4]{0,1:T(4,128)} %param.7) | copy-start | bytes 3076
  431.4 31.4 %all-to-all-start = ((f32[16,1,16384]{2,1,0:T(1,128)}), f32[16,1,16384]{2,1,0:T(1,128)S(1)}, u32[]{:S(2)}, u32[]{:S(2)}) async-start(f32[16,1,16384]{2,1,0:T(1,128)} %reshape.534), calls=%async_computation | async-start | bytes 2097152 | tf_op jit(solution)/shard_map/all_to_all | solution.py:127
  474.4 6.9 %copy-start.11 = (f32[8,300,300]{2,1,0:T(8,128)S(1)}, f32[8,300,300]{2,1,0:T(8,128)}, u32[]{:S(2)}) copy-start(f32[8,300,300]{2,1,0:T(8,128)} %all-gather.2.cloned.1.call-done) | copy-start | bytes 8640004
  484.5 19.2 %collective-permute-start.1 = (f32[64,3,300]{2,1,0:T(4,128)S(1)}, f32[64,3,300]{2,1,0:T(4,128)S(1)}, u32[]{:S(2)}, u32[]{:S(2)}) collective-permute-start(f32[64,3,300]{2,1,0:T(4,128)S(1)} %get-tuple-element.46), channel_id=1, source_target_pairs={{2,0},{4,2},{6,4},{8,6},{10,8},{12,10},{14,12},{16,14},{18,16},{20... | collective-permute-start | bytes 691208 | tf_op jit(solution)/shard_map/ppermute | solution.py:24
  486.4 17.3 %collective-permute-start = (f32[64,3,300]{2,1,0:T(4,128)S(1)}, f32[64,3,300]{2,1,0:T(4,128)S(1)}, u32[]{:S(2)}, u32[]{:S(2)}) collective-permute-start(f32[64,3,300]{2,1,0:T(4,128)S(1)} %get-tuple-element.45), channel_id=1, source_target_pairs={{0,2},{2,4},{4,6},{6,8},{8,10},{10,12},{12,14},{14,16},{16,18},{18... | collective-permute-start | bytes 691208 | tf_op jit(solution)/shard_map/ppermute | solution.py:22
  503.7 6.6 %collective-permute-start.3 = (f32[3,10,300]{2,1,0:T(8,128)S(1)}, f32[3,10,300]{2,1,0:T(8,128)S(1)}, u32[]{:S(2)}, u32[]{:S(2)}) collective-permute-start(f32[3,10,300]{2,1,0:T(8,128)S(1)} %get-tuple-element.42), channel_id=1, source_target_pairs={{1,0},{3,2},{5,4},{7,6},{9,8},{11,10},{13,12},{15,14},{17,16},{19,... | collective-permute-start | bytes 108008 | tf_op jit(solution)/shard_map/ppermute | solution.py:24
  508.3 3.2 collective-permute-start.2
Sparse Core Ops, SparseCore 0:
  365.0 14.8 all-gather.1
